TPU v7x, 256 devices: a whole 4x4x8 slice. The times are simulated.
256 devices in a mesh: shot: 16 (over z, y_lo), xy: 16 (over y_hi, x, core).
Axes of the slice: x: 4, y: 4 (y_hi: 2, y_lo: 2; y = y_hi * 2 + y_lo), z: 8, core: 2. Of those that a mesh axis runs over, the one named last changes fastest.
Arguments:
- fwd_prev: float32 [16, 128, 512, 128], P('shot', 'xy'), may hold values from -6 to 6
- fwd_cur: float32 [16, 128, 512, 128], P('shot', 'xy'), may hold values from -6 to 6
- bwd_next: float32 [16, 128, 512, 128], P('shot', 'xy'), may hold values from -6 to 6
- bwd_cur: float32 [16, 128, 512, 128], P('shot', 'xy'), may hold values from -6 to 6
- receiver_data: float32 [16, 7, 128, 512], P('shot', None, 'xy'), may hold values from -12 to 12
- velocity_term: float32 [128, 512, 128], P('xy'), may hold values from 0.05 to 0.25
- anisotropy: float32 [128, 512, 128], P('xy'), may hold values from 0 to 0.3
- wavelet: float32 [16, 7], replicated, may hold values from -16 to 16
- shot_x: int32 [16], replicated, may hold values from 0 to 127
- shot_y: int32 [16], replicated, may hold values from 0 to 511
- aperture: int32 [16, 8], replicated, may hold values from 0 to 15, all different within a row
- snap_steps: int32 [4], replicated, may hold values from 1 to 8, as said below
Outputs:
- image: float32 [128, 512, 128], P('xy', 'shot')
Inputs may be any that keep to these rules, and one draw needn't show every extreme that they name: `snap_steps`: 4 distinct increasing times; the last is 8. `aperture`: each row names 8 distinct tiles.
All inputs are finite; a program needn't handle non-finite values.
Results may differ from a plain program's by a relative error of at most 0.0021.
Values may be sent and summed in bfloat16 or wider, within the bound.
A program may use at most 128 MiB of HBM per device.

v0:
```python
import jax
import jax.numpy as jnp
from jax import lax
from jax.sharding import PartitionSpec as P


def padded_2(x, sides, width):
    for axis, dim in sides:
        devices, length = (lax.axis_size(axis), x.shape[dim])
        up = [(i, (i + 1) % devices) for i in range(devices - 1)]
        down = [(j, i) for i, j in up]
        last = lax.slice_in_dim(x, length - width, length, axis=dim)
        initial = lax.slice_in_dim(x, 0, width, axis=dim)
        before = lax.ppermute(last, axis, up)
        after = lax.ppermute(initial, axis, down)
        x = jnp.concatenate([before, x, after], axis=dim)
    return x


def passed_along(block, axis, distance):
    devices = range(lax.axis_size(axis))
    route = [((i - distance) % len(devices), i) for i in devices]
    return lax.ppermute(block, axis, route)


def laplace(field, horizontal):
    padded = padded_2(field, (("xy", 0),), 1)
    lateral = padded[2:] + padded[:-2] - 4.0 * field
    side = jnp.pad(field, ((0, 0), (1, 1), (0, 0)))
    lateral = lateral + side[:, 2:] + side[:, :-2]
    deeper = jnp.pad(field, ((0, 0), (0, 0), (1, 1)))
    vertical = deeper[:, :, 2:] + deeper[:, :, :-2] - 2.0 * field
    return horizontal * lateral + vertical


def on_device(
    fwd_prev,
    fwd_cur,
    bwd_next,
    bwd_cur,
    receiver_data,
    velocity_term,
    anisotropy,
    wavelet,
    shot_x,
    shot_y,
    aperture,
    snap_steps,
):
    shot_count = lax.axis_size("shot")
    my_shot = lax.axis_index("shot")
    tile_index = lax.axis_index("xy")
    width = fwd_prev.shape[1]
    depth_cells = fwd_prev.shape[3]
    lateral_cells = fwd_prev.shape[2]
    snap_count = snap_steps.shape[0]
    step_count = wavelet.shape[1] + 1
    half = shot_count // 2
    horizontal = 1.0 + 2.0 * anisotropy
    surface = velocity_term[:, :, 0]
    slots = jnp.arange(snap_count, dtype=jnp.int32)
    shot_ids = jnp.arange(shot_count, dtype=jnp.int32)
    lateral_ids = jnp.arange(lateral_cells, dtype=jnp.int32)

    def record(snaps, field, time):
        is_hit = snap_steps == time
        found = jnp.any(is_hit)
        slot = jnp.sum(jnp.where(is_hit, slots, 0))
        older = lax.dynamic_slice_in_dim(snaps, slot, 1, 0)
        newer = jnp.where(found, field.astype(jnp.bfloat16)[None], older)
        return lax.dynamic_update_slice_in_dim(snaps, newer, slot, 0)

    selected = shot_ids == my_shot
    source_x = jnp.sum(jnp.where(selected, shot_x, 0))
    source_y = jnp.sum(jnp.where(selected, shot_y, 0))
    amplitudes = jnp.sum(jnp.where(selected[:, None], wavelet, 0.0), axis=0)
    cell_x = tile_index * width + jnp.arange(width, dtype=jnp.int32)
    plane = ((cell_x == source_x)[:, None] & (lateral_ids == source_y)[None, :]).astype(jnp.float32)
    source_plane = surface * plane

    def march(before, current, state, visit, source_at):

        def one_step(index, carry):
            before, current, state = carry
            state = visit(state, current, index)
            after = 2.0 * current - before + velocity_term * laplace(current, horizontal)
            after = after.at[:, :, 0].add(source_at(index, False))
            return (current, after, state)

        return lax.fori_loop(0, step_count - 1, one_step, (before, current, state))

    def forward_visit(snaps, field, index):
        return record(snaps, field, index + 1)

    def forward_source(index, widened):
        return source_plane * amplitudes[index]

    empty_snaps = jnp.zeros((snap_count, width, lateral_cells, depth_cells), jnp.bfloat16)
    before, current, snaps = march(
        fwd_prev[0], fwd_cur[0], empty_snaps, forward_visit, forward_source
    )
    snaps = record(snaps, current, step_count)
    snaps = passed_along(snaps, "shot", half)
    image_shot = (my_shot - half) % shot_count
    later, wave, records = (bwd_next[0], bwd_cur[0], receiver_data[0])

    def correlate(partial_value, field, time):
        is_hit = snap_steps == time
        found = jnp.any(is_hit)
        slot = jnp.sum(jnp.where(is_hit, slots, 0))
        taken = lax.dynamic_index_in_dim(snaps, slot, 0, keepdims=False).astype(jnp.float32)
        return partial_value + jnp.where(found, taken * field, 0.0)

    def backward_visit(partial_value, field, index):
        return correlate(partial_value, field, step_count - index)

    def backward_source(index, widened):
        time = step_count - index
        trace = lax.dynamic_index_in_dim(records, time - 2, 0, keepdims=False)
        return surface * trace

    partial_value = jnp.zeros((width, lateral_cells, depth_cells), jnp.float32)
    later, wave, partial_value = march(later, wave, partial_value, backward_visit, backward_source)
    partial_value = correlate(partial_value, wave, 1)
    image_row = jnp.sum(jnp.where((shot_ids == image_shot)[:, None], aperture, 0), axis=0)
    inside = jnp.any(image_row == tile_index).astype(jnp.float32)
    return lax.psum_scatter(partial_value * inside, "shot", scatter_dimension=1, tiled=True)


def solution(mesh):
    in_specs = (
        P("shot", "xy", None, None),
        P("shot", "xy", None, None),
        P("shot", "xy", None, None),
        P("shot", "xy", None, None),
        P("shot", None, "xy", None),
        P("xy", None, None),
        P("xy", None, None),
        P(),
        P(),
        P(),
        P(),
        P(),
    )
    out_specs = P("xy", "shot", None)
    return jax.shard_map(
        on_device, mesh=mesh, in_specs=in_specs, out_specs=out_specs, check_vma=False
    )
```

profile of v0, /device:TPU:40, one launch (start us, length us, event | category | flops | bytes accessed | tf_op | source)
XLA Modules:
  0.0 692.9 jit_solution(9981673842479555574)
XLA Ops:
  29.3 176.5 %while.44 = (s32[]{:T(128)}, f32[8,512,128]{1,0,2:T(8,128)}, f32[8,512,128]{1,0,2:T(8,128)S(1)}, bf16[4,8,512,128]{3,2,1,0:T(8,128)(2,1)}, f32[8,512,128]{1,0,2:...) while((s32[]{:T(128)}, f32[8,512,128]{1,0,2:T(8,128)}, ...), condition=%wide.region_6.7_spmd.clone, body=%wide.region_3.6_spmd.clone.sunk | while | flops 8921111 | bytes 43565388 | solution.py:90
  46.2 4.0 fusion.43
  53.5 4.3 collective-permute-start
  71.8 4.0 fusion.43
  79.1 4.3 collective-permute-start
  97.4 4.0 fusion.43
  104.7 4.3 collective-permute-start
  122.9 4.0 fusion.43
  130.2 4.3 collective-permute-start
  148.5 4.0 fusion.43
  155.8 4.3 collective-permute-start
  174.1 4.0 fusion.43
  181.4 4.3 collective-permute-start
  199.6 4.0 fusion.43
  210.6 6.3 collective-permute-start.4
  225.5 161.8 %collective-permute-done.4 = bf16[4,8,512,128]{3,2,1,0:T(8,128)(2,1)} collective-permute-done((bf16[4,8,512,128]{3,2,1,0:T(8,128)(2,1)}, bf16[4,8,512,128]{3,2,1,0:T(8,128)(2,1)}, u32[]{:S(2)}, u32[]{:S(2)}) %collective-permute-start.4) | collective-permute-done | bytes 4194336 | tf_op jit(solution)/shard_map/ppermute | solution.py:23
  387.3 183.3 %while.45 = (s32[]{:T(128)}, f32[8,512,128]{1,0,2:T(8,128)}, f32[8,512,128]{1,0,2:T(8,128)S(1)}, f32[8,512,128]{1,0,2:T(8,128)}, f32[8,512,128]{1,0,2:T(8,128)},...) while((s32[]{:T(128)}, f32[8,512,128]{1,0,2:T(8,128)}, ...), condition=%wide.region_12.13_spmd.clone, body=%wide.region_9.12_spmd.clone.sunk | while | flops 10493981 | bytes 32047488 | solution.py:90
  388.4 5.5 collective-permute-start.2
  402.5 6.2 fusion.48
  424.3 6.5 fusion.48
  434.2 8.7 %collective-permute-start.2 = (f32[1,512,128]{1,0,2:T(1,128)}, f32[1,512,128]{1,0,2:T(1,128)S(1)}, u32[]{:S(2)}, u32[]{:S(2)}) collective-permute-start(f32[1,512,128]{1,0,2:T(1,128)} %get-tuple-element.892), channel_id=1, source_target_pairs={{0,1},{1,2},{2,3},{3,4},{4,5},{5,6},{6,7},{7,8},{8,9},{9,10},{10,1... | collective-permute-start | bytes 786440 | tf_op jit(solution)/shard_map/while/body/eval_jaxpr/ppermute | solution.py:14
  451.5 6.5 fusion.48
  461.4 10.3 %collective-permute-start.2 = (f32[1,512,128]{1,0,2:T(1,128)}, f32[1,512,128]{1,0,2:T(1,128)S(1)}, u32[]{:S(2)}, u32[]{:S(2)}) collective-permute-start(f32[1,512,128]{1,0,2:T(1,128)} %get-tuple-element.892), channel_id=1, source_target_pairs={{0,1},{1,2},{2,3},{3,4},{4,5},{5,6},{6,7},{7,8},{8,9},{9,10},{10,1... | collective-permute-start | bytes 786440 | tf_op jit(solution)/shard_map/while/body/eval_jaxpr/ppermute | solution.py:14
  480.3 6.5 fusion.48
  490.2 10.3 %collective-permute-start.2 = (f32[1,512,128]{1,0,2:T(1,128)}, f32[1,512,128]{1,0,2:T(1,128)S(1)}, u32[]{:S(2)}, u32[]{:S(2)}) collective-permute-start(f32[1,512,128]{1,0,2:T(1,128)} %get-tuple-element.892), channel_id=1, source_target_pairs={{0,1},{1,2},{2,3},{3,4},{4,5},{5,6},{6,7},{7,8},{8,9},{9,10},{10,1... | collective-permute-start | bytes 786440 | tf_op jit(solution)/shard_map/while/body/eval_jaxpr/ppermute | solution.py:14
  509.1 6.5 fusion.48
  519.0 7.9 %collective-permute-start.2 = (f32[1,512,128]{1,0,2:T(1,128)}, f32[1,512,128]{1,0,2:T(1,128)S(1)}, u32[]{:S(2)}, u32[]{:S(2)}) collective-permute-start(f32[1,512,128]{1,0,2:T(1,128)} %get-tuple-element.892), channel_id=1, source_target_pairs={{0,1},{1,2},{2,3},{3,4},{4,5},{5,6},{6,7},{7,8},{8,9},{9,10},{10,1... | collective-permute-start | bytes 786440 | tf_op jit(solution)/shard_map/while/body/eval_jaxpr/ppermute | solution.py:14
  535.4 6.5 fusion.48
  545.3 7.9 %collective-permute-start.2 = (f32[1,512,128]{1,0,2:T(1,128)}, f32[1,512,128]{1,0,2:T(1,128)S(1)}, u32[]{:S(2)}, u32[]{:S(2)}) collective-permute-start(f32[1,512,128]{1,0,2:T(1,128)} %get-tuple-element.892), channel_id=1, source_target_pairs={{0,1},{1,2},{2,3},{3,4},{4,5},{5,6},{6,7},{7,8},{8,9},{9,10},{10,1... | collective-permute-start | bytes 786440 | tf_op jit(solution)/shard_map/while/body/eval_jaxpr/ppermute | solution.py:14
  561.8 6.5 fusion.48
  575.6 4.1 fusion.28
  579.7 106.3 %reduce-scatter.2.cloned.1.call-done = f32[8,32,128]{2,1,0:T(8,128)} async-done(((f32[8,512,128]{2,1,0:T(8,128)}), f32[8,32,128]{2,1,0:T(8,128)}) %reduce-scatter.2.cloned.1.call-update) | async-done | bytes 131088 | tf_op jit(solution)/shard_map/reduce_scatter | solution.py:127
  (235 shorter events, 220.3 us)
Async XLA Ops:
  6.5 679.5 %reduce-scatter.2.cloned.1.call-start = ((), (), s32[]{:S(2)}) async-start(), calls=%async_computation.1 | async-start | bytes 2228224 | tf_op jit(solution)/shard_map/reduce_scatter | solution.py:127
  30.4 15.7 %collective-permute-start = (f32[1,512,128]{1,0,2:T(1,128)}, f32[1,512,128]{1,0,2:T(1,128)S(1)}, u32[]{:S(2)}, u32[]{:S(2)}) collective-permute-start(f32[1,512,128]{1,0,2:T(1,128)} %get-tuple-element.880), channel_id=1, source_target_pairs={{0,1},{1,2},{2,3},{3,4},{4,5},{5,6},{6,7},{7,8},{8,9},{9,10},{10,1... | collective-permute-start | bytes 786440 | tf_op jit(solution)/shard_map/while/body/eval_jaxpr/ppermute | solution.py:14
  32.2 14.0 %collective-permute-start.1 = (f32[1,512,128]{1,0,2:T(1,128)}, f32[1,512,128]{1,0,2:T(1,128)}, u32[]{:S(2)}, u32[]{:S(2)}) collective-permute-start(f32[1,512,128]{1,0,2:T(1,128)} %get-tuple-element.881), channel_id=1, source_target_pairs={{1,0},{2,1},{3,2},{4,3},{5,4},{6,5},{7,6},{8,7},{9,8},{10,9},{11,1... | collective-permute-start | bytes 786440 | tf_op jit(solution)/shard_map/while/body/eval_jaxpr/ppermute | solution.py:15
  53.5 18.3 %collective-permute-start = (f32[1,512,128]{1,0,2:T(1,128)}, f32[1,512,128]{1,0,2:T(1,128)S(1)}, u32[]{:S(2)}, u32[]{:S(2)}) collective-permute-start(f32[1,512,128]{1,0,2:T(1,128)} %get-tuple-element.880), channel_id=1, source_target_pairs={{0,1},{1,2},{2,3},{3,4},{4,5},{5,6},{6,7},{7,8},{8,9},{9,10},{10,1... | collective-permute-start | bytes 786440 | tf_op jit(solution)/shard_map/while/body/eval_jaxpr/ppermute | solution.py:14
  57.8 14.0 %collective-permute-start.1 = (f32[1,512,128]{1,0,2:T(1,128)}, f32[1,512,128]{1,0,2:T(1,128)}, u32[]{:S(2)}, u32[]{:S(2)}) collective-permute-start(f32[1,512,128]{1,0,2:T(1,128)} %get-tuple-element.881), channel_id=1, source_target_pairs={{1,0},{2,1},{3,2},{4,3},{5,4},{6,5},{7,6},{8,7},{9,8},{10,9},{11,1... | collective-permute-start | bytes 786440 | tf_op jit(solution)/shard_map/while/body/eval_jaxpr/ppermute | solution.py:15
  79.1 18.3 %collective-permute-start = (f32[1,512,128]{1,0,2:T(1,128)}, f32[1,512,128]{1,0,2:T(1,128)S(1)}, u32[]{:S(2)}, u32[]{:S(2)}) collective-permute-start(f32[1,512,128]{1,0,2:T(1,128)} %get-tuple-element.880), channel_id=1, source_target_pairs={{0,1},{1,2},{2,3},{3,4},{4,5},{5,6},{6,7},{7,8},{8,9},{9,10},{10,1... | collective-permute-start | bytes 786440 | tf_op jit(solution)/shard_map/while/body/eval_jaxpr/ppermute | solution.py:14
  83.4 14.0 %collective-permute-start.1 = (f32[1,512,128]{1,0,2:T(1,128)}, f32[1,512,128]{1,0,2:T(1,128)}, u32[]{:S(2)}, u32[]{:S(2)}) collective-permute-start(f32[1,512,128]{1,0,2:T(1,128)} %get-tuple-element.881), channel_id=1, source_target_pairs={{1,0},{2,1},{3,2},{4,3},{5,4},{6,5},{7,6},{8,7},{9,8},{10,9},{11,1... | collective-permute-start | bytes 786440 | tf_op jit(solution)/shard_map/while/body/eval_jaxpr/ppermute | solution.py:15
  104.7 18.3 %collective-permute-start = (f32[1,512,128]{1,0,2:T(1,128)}, f32[1,512,128]{1,0,2:T(1,128)S(1)}, u32[]{:S(2)}, u32[]{:S(2)}) collective-permute-start(f32[1,512,128]{1,0,2:T(1,128)} %get-tuple-element.880), channel_id=1, source_target_pairs={{0,1},{1,2},{2,3},{3,4},{4,5},{5,6},{6,7},{7,8},{8,9},{9,10},{10,1... | collective-permute-start | bytes 786440 | tf_op jit(solution)/shard_map/while/body/eval_jaxpr/ppermute | solution.py:14
  108.9 14.0 %collective-permute-start.1 = (f32[1,512,128]{1,0,2:T(1,128)}, f32[1,512,128]{1,0,2:T(1,128)}, u32[]{:S(2)}, u32[]{:S(2)}) collective-permute-start(f32[1,512,128]{1,0,2:T(1,128)} %get-tuple-element.881), channel_id=1, source_target_pairs={{1,0},{2,1},{3,2},{4,3},{5,4},{6,5},{7,6},{8,7},{9,8},{10,9},{11,1... | collective-permute-start | bytes 786440 | tf_op jit(solution)/shard_map/while/body/eval_jaxpr/ppermute | solution.py:15
  130.2 18.3 %collective-permute-start = (f32[1,512,128]{1,0,2:T(1,128)}, f32[1,512,128]{1,0,2:T(1,128)S(1)}, u32[]{:S(2)}, u32[]{:S(2)}) collective-permute-start(f32[1,512,128]{1,0,2:T(1,128)} %get-tuple-element.880), channel_id=1, source_target_pairs={{0,1},{1,2},{2,3},{3,4},{4,5},{5,6},{6,7},{7,8},{8,9},{9,10},{10,1... | collective-permute-start | bytes 786440 | tf_op jit(solution)/shard_map/while/body/eval_jaxpr/ppermute | solution.py:14
  134.5 14.0 %collective-permute-start.1 = (f32[1,512,128]{1,0,2:T(1,128)}, f32[1,512,128]{1,0,2:T(1,128)}, u32[]{:S(2)}, u32[]{:S(2)}) collective-permute-start(f32[1,512,128]{1,0,2:T(1,128)} %get-tuple-element.881), channel_id=1, source_target_pairs={{1,0},{2,1},{3,2},{4,3},{5,4},{6,5},{7,6},{8,7},{9,8},{10,9},{11,1... | collective-permute-start | bytes 786440 | tf_op jit(solution)/shard_map/while/body/eval_jaxpr/ppermute | solution.py:15
  155.8 18.3 %collective-permute-start = (f32[1,512,128]{1,0,2:T(1,128)}, f32[1,512,128]{1,0,2:T(1,128)S(1)}, u32[]{:S(2)}, u32[]{:S(2)}) collective-permute-start(f32[1,512,128]{1,0,2:T(1,128)} %get-tuple-element.880), channel_id=1, source_target_pairs={{0,1},{1,2},{2,3},{3,4},{4,5},{5,6},{6,7},{7,8},{8,9},{9,10},{10,1... | collective-permute-start | bytes 786440 | tf_op jit(solution)/shard_map/while/body/eval_jaxpr/ppermute | solution.py:14
  160.0 14.0 %collective-permute-start.1 = (f32[1,512,128]{1,0,2:T(1,128)}, f32[1,512,128]{1,0,2:T(1,128)}, u32[]{:S(2)}, u32[]{:S(2)}) collective-permute-start(f32[1,512,128]{1,0,2:T(1,128)} %get-tuple-element.881), channel_id=1, source_target_pairs={{1,0},{2,1},{3,2},{4,3},{5,4},{6,5},{7,6},{8,7},{9,8},{10,9},{11,1... | collective-permute-start | bytes 786440 | tf_op jit(solution)/shard_map/while/body/eval_jaxpr/ppermute | solution.py:15
  181.4 18.3 %collective-permute-start = (f32[1,512,128]{1,0,2:T(1,128)}, f32[1,512,128]{1,0,2:T(1,128)S(1)}, u32[]{:S(2)}, u32[]{:S(2)}) collective-permute-start(f32[1,512,128]{1,0,2:T(1,128)} %get-tuple-element.880), channel_id=1, source_target_pairs={{0,1},{1,2},{2,3},{3,4},{4,5},{5,6},{6,7},{7,8},{8,9},{9,10},{10,1... | collective-permute-start | bytes 786440 | tf_op jit(solution)/shard_map/while/body/eval_jaxpr/ppermute | solution.py:14
  185.6 14.0 %collective-permute-start.1 = (f32[1,512,128]{1,0,2:T(1,128)}, f32[1,512,128]{1,0,2:T(1,128)}, u32[]{:S(2)}, u32[]{:S(2)}) collective-permute-start(f32[1,512,128]{1,0,2:T(1,128)} %get-tuple-element.881), channel_id=1, source_target_pairs={{1,0},{2,1},{3,2},{4,3},{5,4},{6,5},{7,6},{8,7},{9,8},{10,9},{11,1... | collective-permute-start | bytes 786440 | tf_op jit(solution)/shard_map/while/body/eval_jaxpr/ppermute | solution.py:15
  206.7 11.6 %copy-start.4 = (s32[16,8]{0,1:T(8,128)S(1)}, s32[16,8]{0,1:T(8,128)}, u32[]{:S(2)}) copy-start(s32[16,8]{0,1:T(8,128)} %param.30) | copy-start | bytes 1540
  206.8 13.1 %copy-start.2 = (f32[1,8,512,128]{3,2,1,0:T(8,128)S(1)}, f32[1,8,512,128]{3,2,1,0:T(8,128)}, u32[]{:S(2)}) copy-start(f32[1,8,512,128]{3,2,1,0:T(8,128)} %param.22) | copy-start | bytes 6291460
  210.6 176.6 %collective-permute-start.4 = (bf16[4,8,512,128]{3,2,1,0:T(8,128)(2,1)}, bf16[4,8,512,128]{3,2,1,0:T(8,128)(2,1)}, u32[]{:S(2)}, u32[]{:S(2)}) collective-permute-start(bf16[4,8,512,128]{3,2,1,0:T(8,128)(2,1)} %fusion.29), channel_id=1, source_target_pairs={{128,0},{144,16},{160,32},{176,48},{192,64},{208,80},{224,96},{240... | collective-permute-start | bytes 12582920 | tf_op jit(solution)/shard_map/ppermute | solution.py:23
  388.4 14.1 %collective-permute-start.2 = (f32[1,512,128]{1,0,2:T(1,128)}, f32[1,512,128]{1,0,2:T(1,128)S(1)}, u32[]{:S(2)}, u32[]{:S(2)}) collective-permute-start(f32[1,512,128]{1,0,2:T(1,128)} %get-tuple-element.892), channel_id=1, source_target_pairs={{0,1},{1,2},{2,3},{3,4},{4,5},{5,6},{6,7},{7,8},{8,9},{9,10},{10,1... | collective-permute-start | bytes 786440 | tf_op jit(solution)/shard_map/while/body/eval_jaxpr/ppermute | solution.py:14
  393.9 8.6 %collective-permute-start.3 = (f32[1,512,128]{1,0,2:T(1,128)}, f32[1,512,128]{1,0,2:T(1,128)}, u32[]{:S(2)}, u32[]{:S(2)}) collective-permute-start(f32[1,512,128]{1,0,2:T(1,128)} %get-tuple-element.893), channel_id=1, source_target_pairs={{1,0},{2,1},{3,2},{4,3},{5,4},{6,5},{7,6},{8,7},{9,8},{10,9},{11,1... | collective-permute-start | bytes 786440 | tf_op jit(solution)/shard_map/while/body/eval_jaxpr/ppermute | solution.py:15
  412.1 12.3 %collective-permute-start.2 = (f32[1,512,128]{1,0,2:T(1,128)}, f32[1,512,128]{1,0,2:T(1,128)S(1)}, u32[]{:S(2)}, u32[]{:S(2)}) collective-permute-start(f32[1,512,128]{1,0,2:T(1,128)} %get-tuple-element.892), channel_id=1, source_target_pairs={{0,1},{1,2},{2,3},{3,4},{4,5},{5,6},{6,7},{7,8},{8,9},{9,10},{10,1... | collective-permute-start | bytes 786440 | tf_op jit(solution)/shard_map/while/body/eval_jaxpr/ppermute | solution.py:14
  415.7 8.6 %collective-permute-start.3 = (f32[1,512,128]{1,0,2:T(1,128)}, f32[1,512,128]{1,0,2:T(1,128)}, u32[]{:S(2)}, u32[]{:S(2)}) collective-permute-start(f32[1,512,128]{1,0,2:T(1,128)} %get-tuple-element.893), channel_id=1, source_target_pairs={{1,0},{2,1},{3,2},{4,3},{5,4},{6,5},{7,6},{8,7},{9,8},{10,9},{11,1... | collective-permute-start | bytes 786440 | tf_op jit(solution)/shard_map/while/body/eval_jaxpr/ppermute | solution.py:15
  434.2 17.3 %collective-permute-start.2 = (f32[1,512,128]{1,0,2:T(1,128)}, f32[1,512,128]{1,0,2:T(1,128)S(1)}, u32[]{:S(2)}, u32[]{:S(2)}) collective-permute-start(f32[1,512,128]{1,0,2:T(1,128)} %get-tuple-element.892), channel_id=1, source_target_pairs={{0,1},{1,2},{2,3},{3,4},{4,5},{5,6},{6,7},{7,8},{8,9},{9,10},{10,1... | collective-permute-start | bytes 786440 | tf_op jit(solution)/shard_map/while/body/eval_jaxpr/ppermute | solution.py:14
  442.9 8.6 %collective-permute-start.3 = (f32[1,512,128]{1,0,2:T(1,128)}, f32[1,512,128]{1,0,2:T(1,128)}, u32[]{:S(2)}, u32[]{:S(2)}) collective-permute-start(f32[1,512,128]{1,0,2:T(1,128)} %get-tuple-element.893), channel_id=1, source_target_pairs={{1,0},{2,1},{3,2},{4,3},{5,4},{6,5},{7,6},{8,7},{9,8},{10,9},{11,1... | collective-permute-start | bytes 786440 | tf_op jit(solution)/shard_map/while/body/eval_jaxpr/ppermute | solution.py:15
  461.4 18.9 %collective-permute-start.2 = (f32[1,512,128]{1,0,2:T(1,128)}, f32[1,512,128]{1,0,2:T(1,128)S(1)}, u32[]{:S(2)}, u32[]{:S(2)}) collective-permute-start(f32[1,512,128]{1,0,2:T(1,128)} %get-tuple-element.892), channel_id=1, source_target_pairs={{0,1},{1,2},{2,3},{3,4},{4,5},{5,6},{6,7},{7,8},{8,9},{9,10},{10,1... | collective-permute-start | bytes 786440 | tf_op jit(solution)/shard_map/while/body/eval_jaxpr/ppermute | solution.py:14
  471.7 8.6 %collective-permute-start.3 = (f32[1,512,128]{1,0,2:T(1,128)}, f32[1,512,128]{1,0,2:T(1,128)}, u32[]{:S(2)}, u32[]{:S(2)}) collective-permute-start(f32[1,512,128]{1,0,2:T(1,128)} %get-tuple-element.893), channel_id=1, source_target_pairs={{1,0},{2,1},{3,2},{4,3},{5,4},{6,5},{7,6},{8,7},{9,8},{10,9},{11,1... | collective-permute-start | bytes 786440 | tf_op jit(solution)/shard_map/while/body/eval_jaxpr/ppermute | solution.py:15
  490.2 18.9 %collective-permute-start.2 = (f32[1,512,128]{1,0,2:T(1,128)}, f32[1,512,128]{1,0,2:T(1,128)S(1)}, u32[]{:S(2)}, u32[]{:S(2)}) collective-permute-start(f32[1,512,128]{1,0,2:T(1,128)} %get-tuple-element.892), channel_id=1, source_target_pairs={{0,1},{1,2},{2,3},{3,4},{4,5},{5,6},{6,7},{7,8},{8,9},{9,10},{10,1... | collective-permute-start | bytes 786440 | tf_op jit(solution)/shard_map/while/body/eval_jaxpr/ppermute | solution.py:14
  500.5 8.6 %collective-permute-start.3 = (f32[1,512,128]{1,0,2:T(1,128)}, f32[1,512,128]{1,0,2:T(1,128)}, u32[]{:S(2)}, u32[]{:S(2)}) collective-permute-start(f32[1,512,128]{1,0,2:T(1,128)} %get-tuple-element.893), channel_id=1, source_target_pairs={{1,0},{2,1},{3,2},{4,3},{5,4},{6,5},{7,6},{8,7},{9,8},{10,9},{11,1... | collective-permute-start | bytes 786440 | tf_op jit(solution)/shard_map/while/body/eval_jaxpr/ppermute | solution.py:15
  519.0 16.5 %collective-permute-start.2 = (f32[1,512,128]{1,0,2:T(1,128)}, f32[1,512,128]{1,0,2:T(1,128)S(1)}, u32[]{:S(2)}, u32[]{:S(2)}) collective-permute-start(f32[1,512,128]{1,0,2:T(1,128)} %get-tuple-element.892), channel_id=1, source_target_pairs={{0,1},{1,2},{2,3},{3,4},{4,5},{5,6},{6,7},{7,8},{8,9},{9,10},{10,1... | collective-permute-start | bytes 786440 | tf_op jit(solution)/shard_map/while/body/eval_jaxpr/ppermute | solution.py:14
  526.8 8.6 %collective-permute-start.3 = (f32[1,512,128]{1,0,2:T(1,128)}, f32[1,512,128]{1,0,2:T(1,128)}, u32[]{:S(2)}, u32[]{:S(2)}) collective-permute-start(f32[1,512,128]{1,0,2:T(1,128)} %get-tuple-element.893), channel_id=1, source_target_pairs={{1,0},{2,1},{3,2},{4,3},{5,4},{6,5},{7,6},{8,7},{9,8},{10,9},{11,1... | collective-permute-start | bytes 786440 | tf_op jit(solution)/shard_map/while/body/eval_jaxpr/ppermute | solution.py:15
  545.3 16.5 %collective-permute-start.2 = (f32[1,512,128]{1,0,2:T(1,128)}, f32[1,512,128]{1,0,2:T(1,128)S(1)}, u32[]{:S(2)}, u32[]{:S(2)}) collective-permute-start(f32[1,512,128]{1,0,2:T(1,128)} %get-tuple-element.892), channel_id=1, source_target_pairs={{0,1},{1,2},{2,3},{3,4},{4,5},{5,6},{6,7},{7,8},{8,9},{9,10},{10,1... | collective-permute-start | bytes 786440 | tf_op jit(solution)/shard_map/while/body/eval_jaxpr/ppermute | solution.py:14
  553.2 8.6 %collective-permute-start.3 = (f32[1,512,128]{1,0,2:T(1,128)}, f32[1,512,128]{1,0,2:T(1,128)}, u32[]{:S(2)}, u32[]{:S(2)}) collective-permute-start(f32[1,512,128]{1,0,2:T(1,128)} %get-tuple-element.893), channel_id=1, source_target_pairs={{1,0},{2,1},{3,2},{4,3},{5,4},{6,5},{7,6},{8,7},{9,8},{10,9},{11,1... | collective-permute-start | bytes 786440 | tf_op jit(solution)/shard_map/while/body/eval_jaxpr/ppermute | solution.py:15
  (10 other events, 22.1 us)
Sparse Core Ops, SparseCore 0:
  579.8 106.1 reduce-scatter.1
where the time goes:
time: 701 us; the launch traced here: 693 us
  waiting for transfers between devices  268 us (38%)
  local copies, waits for them, and re-layouts  145 us (21%)
  other arithmetic  129 us (18%)
  starting transfers between devices  106 us (15%)
  loops' own time  26.8 us (4%)
  between operations  18.3 us (3%)
    ppermute x1, waiting for transfers between devices, passed_along(): return lax.ppermute(block, axis, route)  162 us
    reduce_scatter x1, waiting for transfers between devices, on_device(): lax.psum_scatter(partial_value * inside, 'shot', scatter_dimension=1, til...  106 us
    ppermute x14, starting transfers between devices, padded_2(): before = lax.ppermute(last, axis, up)  81.4 us
    add x7, other arithmetic, correlate(): return partial_value + jnp.where(found, taken * field, 0.0)  45.2 us
    dynamic_slice x14, local copies, waits for them, and re-layouts, record(): older = lax.dynamic_slice_in_dim(snaps, slot, 1, 0)  29.1 us
    dynamic_slice x14, local copies, waits for them, and re-layouts, correlate(): lax.dynamic_index_in_dim(snaps, slot, 0, keepdims=False).astype(jnp.float32)  29 us
    add x7, other arithmetic, one_step(): 2.0 * current - before + velocity_term * laplace(current, horizontal)  27.8 us
    another operation x2, loops' own time, march(): return lax.fori_loop(0, step_count - 1, one_step, (before, current, state))  26.8 us
  transfers between devices with their start and end apart: 30, of which 2 were waited for; matrix products, arithmetic and copies ran while one was open for 17% of the time, Pallas kernels for 0%

commit v1 on v0

v1 whole, which is shorter than its diff:
```python
import functools

import jax
import jax.numpy as jnp
from jax import lax
from jax.experimental import pallas as pl
from jax.experimental.pallas import tpu as pltpu
from jax.sharding import PartitionSpec as P

MESH = pl.DeviceIdType.MESH
TOP = 32767.0
BLOCKS = 33
CHUNK = 3
CHUNKS = BLOCKS // CHUNK
ROWS = 8 * BLOCKS
STEPS = 7
WIDE = 22
FIELD_TOP = 6.0
RECORD_TOP = 12.0
SPEED_TOP = 0.25
SHAPE_TOP = 0.3


def root_code(x, top):
    size = jnp.sqrt(jnp.sqrt(jnp.abs(x) * (1.0 / top))) * TOP
    size = jnp.minimum(jnp.round(size), TOP)
    return jnp.where(x < 0.0, -size, size).astype(jnp.int32).astype(jnp.int16)


def root_value(code, top):
    part = code.astype(jnp.int32).astype(jnp.float32) * (1.0 / TOP)
    return (part * part) * (part * jnp.abs(part)) * top


def line_code(x, top):
    return jnp.round(x * (TOP / top)).astype(jnp.int32).astype(jnp.int16)


def line_value(code, top):
    return code.astype(jnp.int32).astype(jnp.float32) * (top / TOP)


def kernel(
    fields0, fields1, fields2, fields3, speed_hbm, shape_hbm, records, wavelet, shot_x, shot_y, aperture, snap_steps,
    out,
    state, slope, speed, snap_u, snap_w, total, stage, z_out, z_in, near, near_in, far_in,
    inject, marks, turned, rec_z, rec_near, rec_z_in, rec_near_in, rec_far_in, sums,
    in_sem, z_send, z_recv, near_send, near_recv, far_send, far_recv,
    rz_send, rz_recv, rn_send, rn_recv, rf_send, rf_recv, sum_send, sum_recv,
):
    fields = (fields0, fields1, fields2, fields3)
    s, q = lax.axis_index("shot"), lax.axis_index("xy")
    half = s // 8
    across = lax.rem(s + 8, 16)
    left, right = lax.rem(q + 15, 16), lax.rem(q + 1, 16)
    sides = ((s, left), (s, right))
    base = pl.multiple_of(248 * half, 8)
    their_base = pl.multiple_of(248 * (1 - half), 8)

    loads = []
    for f in range(4):
        loads.append(pltpu.make_async_copy(fields[f].at[0, :, pl.ds(their_base, ROWS), :], stage.at[f], in_sem.at[f]))
    for f in range(4):
        loads.append(pltpu.make_async_copy(fields[f].at[0, :, pl.ds(base, ROWS), :], state.at[f, pl.ds(7, 8), pl.ds(8, ROWS), :], in_sem.at[4 + f]))
    loads.append(pltpu.make_async_copy(shape_hbm.at[:, pl.ds(base, ROWS), :], slope.at[pl.ds(7, 8)], in_sem.at[8]))
    loads.append(pltpu.make_async_copy(speed_hbm.at[:, pl.ds(base, ROWS), :], speed.at[pl.ds(7, 8)], in_sem.at[9]))
    for load in loads:
        load.start()

    barrier = pltpu.get_barrier_semaphore()
    peers = [(across, q), *sides]
    for k in range(1, 8):
        peers.append((8 * half + lax.rem(s + k, 8), q))
    for peer in peers:
        pl.semaphore_signal(barrier, inc=1, device_id=peer, device_id_type=MESH)

    def remote(src, dst, send, recv, target):
        return pltpu.make_async_remote_copy(
            src_ref=src, dst_ref=dst, send_sem=send, recv_sem=recv, device_id=target, device_id_type=MESH
        )

    def z_copy(j):
        return remote(z_out.at[j], z_in.at[j], z_send.at[j], z_recv.at[j], (across, q))

    def near_copy(j, side):
        return remote(near.at[j], near_in.at[1 - side, j], near_send.at[side, j], near_recv.at[1 - side, j], sides[side])

    def far_copy(j, side):
        return remote(z_in.at[j], far_in.at[1 - side, j], far_send.at[side, j], far_recv.at[1 - side, j], sides[side])

    def arrived(copy_of, j, side):
        return copy_of(j, 1 - side)

    def rec_near_copy(side):
        return remote(rec_near, rec_near_in.at[1 - side], rn_send.at[side], rn_recv.at[1 - side], sides[side])

    def rec_far_copy(side):
        return remote(rec_z_in, rec_far_in.at[1 - side], rf_send.at[side], rf_recv.at[1 - side], sides[side])

    rec_z_copy = remote(rec_z, rec_z_in, rz_send, rz_recv, (across, q))

    for load in loads[:4]:
        load.wait()
    pl.semaphore_wait(barrier, len(peers))

    @pl.loop(0, CHUNKS)
    def _(j):
        for f in range(4):
            for i in range(CHUNK):
                row = pl.multiple_of(8 * (CHUNK * j + i), 8)
                block = stage[f, :, pl.ds(row, 8), :].reshape(64, 128)
                z_out[j, CHUNK * f + i] = root_code(block, FIELD_TOP)
        z_copy(j).start()

    for load in loads[4:]:
        load.wait()

    @pl.loop(0, CHUNKS)
    def _(j):
        for i in range(CHUNK):
            row = pl.multiple_of(8 * (CHUNK * j + i), 8)
            for f in range(4):
                block = state[f, 7:15, pl.ds(row + 8, 8), :].reshape(64, 128)
                near[j, CHUNK * f + i] = root_code(block, FIELD_TOP)
            near[j, CHUNK * 4 + i] = line_code(slope[7:15, pl.ds(row, 8), :].reshape(64, 128), SHAPE_TOP)
            near[j, CHUNK * 5 + i] = line_code(speed[7:15, pl.ds(row, 8), :].reshape(64, 128), SPEED_TOP)
        for side in range(2):
            near_copy(j, side).start()

    marks[...] = jnp.zeros_like(marks)
    for t in range(STEPS):
        for x in range(8):
            marks[x, t : t + 1, :] = records[0, t, x : x + 1, :]
    turned[pl.ds(512, 16)] = jnp.zeros((16, 128), jnp.float32)
    turned[pl.ds(0, 512)] = jnp.transpose(marks[...].reshape(128, 512), (1, 0))

    @pl.loop(0, 17)
    def _(k):
        row = 16 * k
        rec_z[k] = root_code(turned[pl.ds(pl.multiple_of(their_base + row, 8), 16), :], RECORD_TOP)
        rec_near[k] = root_code(turned[pl.ds(pl.multiple_of(base + row, 8), 16), :], RECORD_TOP)

    rec_z_copy.start()
    for side in range(2):
        rec_near_copy(side).start()

    lane = lax.broadcasted_iota(jnp.int32, (8, 128), 1)
    sub = lax.broadcasted_iota(jnp.int32, (8, 128), 0)
    wide_lane = lax.broadcasted_iota(jnp.int32, (16, 128), 1)
    has = (jnp.where(q > 0, 1.0, 0.0), jnp.where(q < 15, 1.0, 0.0))

    def fill_source(shot):
        tag = jnp.zeros((8, 128), jnp.float32)
        for t in range(STEPS):
            tag = jnp.where((lane & 7) == t, wavelet[shot, t], tag)
        at_x = shot_x[shot] - 8 * q + 7
        at_y = shot_y[shot] - base

        @pl.loop(0, BLOCKS)
        def _(k):
            row = pl.multiple_of(8 * k, 8)
            for g in range(2):
                hit = ((sub + row) == at_y) & (((lane >> 3) + 16 * g) == at_x)
                inject[0, g, pl.ds(row, 8), :] = jnp.where(hit, tag, 0.0)

    def fill_records(middle, beside):
        @pl.loop(0, 17)
        def _(k):
            row = pl.multiple_of(16 * k, 8)
            low = pltpu.roll(root_value(beside[0, k], RECORD_TOP), 120, 1) * has[0]
            mid = pltpu.roll(root_value(middle[k], RECORD_TOP), 56, 1)
            high = pltpu.roll(root_value(beside[1, k], RECORD_TOP), 120, 1) * has[1]
            inject[1, 0, pl.ds(row, 16), :] = jnp.where(wide_lane < 56, low, jnp.where(wide_lane < 120, mid, high))
            inject[1, 1, pl.ds(row, 16), :] = high

    for f in range(4):
        state[f, :, 0:8, :] = jnp.zeros((WIDE, 8, 128), jnp.float32)
        state[f, :, ROWS + 8 : ROWS + 16, :] = jnp.zeros((WIDE, 8, 128), jnp.float32)

    def imaged(shot):
        inside = jnp.float32(0.0)
        for i in range(8):
            inside = inside + jnp.where(aperture[shot, i] == q, 1.0, 0.0)
        scale = []
        for t in range(1, 9):
            hit = jnp.float32(0.0)
            for i in range(4):
                hit = hit + jnp.where(snap_steps[i] == t, 1.0, 0.0)
            scale.append(hit * inside)
        return scale

    own_scale, other_scale = imaged(s), imaged(across)

    def rounded(x):
        return x.astype(jnp.bfloat16).astype(jnp.float32)

    def one_step(phase, w, n, k):
        old, now = 2 * w + (n - 1) % 2, 2 * w + n % 2
        entry = n - 1 if w == 0 else STEPS - n
        row = pl.multiple_of(8 * k, 8)
        here = pl.ds(pl.multiple_of(row + 8, 8), 8)
        groups = [(7, 15)] if n == STEPS else [(n, 7), (7, 15), (15, WIDE - n)]
        for x0, x1 in groups:
            count = x1 - x0
            big = state[now, x0 - 1 : x1 + 1, here, :]
            mid = big[1:-1]
            lateral = big[:-2] + big[2:]
            lateral = lateral + state[now, x0:x1, pl.ds(row + 7, 8), :]
            lateral = lateral + state[now, x0:x1, pl.ds(row + 9, 8), :]
            lateral = lateral - 4.0 * mid
            sources = [inject[w, g, pl.ds(row, 8), :] for g in range(2)]
            added = jnp.stack([
                pltpu.roll(sources[x // 16], (128 - 8 * (x % 16) - entry) % 128, 1) for x in range(x0, x1)
            ])
            at = lax.broadcasted_iota(jnp.int32, (count, 8, 128), 2)
            up = jnp.where(at == 0, added, pltpu.roll(mid, 1, 2))
            down = jnp.where(at == 127, 0.0, pltpu.roll(mid, 127, 2))
            twice = 2.0 * mid
            vertical = up + down - twice
            new = twice - state[old, x0:x1, here, :]
            new = new + slope[x0:x1, pl.ds(row, 8), :] * lateral + speed[x0:x1, pl.ds(row, 8), :] * vertical
            state[old, x0:x1, here, :] = new
            if x0 == 7:
                flat = new.reshape(64, 128)
                if phase == 0 and w == 0:
                    snap_u[n, k] = flat.astype(jnp.bfloat16)
                elif phase == 0:
                    snap_w[STEPS - n, k] = flat
                elif w == 0:
                    total[k] += other_scale[n] * rounded(flat) * snap_w[n, k]
                else:
                    level = STEPS - n
                    total[k] += own_scale[level] * flat * snap_u[level, k].astype(jnp.float32)

    def spread(f, rows, low, high, mid=None):
        state[f, 0:7, rows, :] = (root_value(low, FIELD_TOP) * has[0]).reshape(8, 8, 128)[1:8]
        state[f, 15:22, rows, :] = (root_value(high, FIELD_TOP) * has[1]).reshape(8, 8, 128)[0:7]
        if mid is not None:
            mid = root_value(mid, FIELD_TOP)
            state[f, 7:15, rows, :] = mid.reshape(8, 8, 128)
        return mid

    def open_near(j):
        @pl.loop(0, CHUNK)
        def _(i):
            k = CHUNK * j + i
            row = pl.multiple_of(8 * k, 8)
            rows = pl.ds(pl.multiple_of(row + 8, 8), 8)
            for f in range(4):
                spread(f, rows, near_in[0, j, CHUNK * f + i], near_in[1, j, CHUNK * f + i])
            snap_u[0, k] = state[1, 7:15, rows, :].reshape(64, 128).astype(jnp.bfloat16)
            snap_w[STEPS, k] = state[3, 7:15, rows, :].reshape(64, 128)
            for side, cut, into in ((0, slice(1, 8), slice(0, 7)), (1, slice(0, 7), slice(15, 22))):
                tilt = line_value(near_in[side, j, CHUNK * 4 + i], SHAPE_TOP)
                fast = line_value(near_in[side, j, CHUNK * 5 + i], SPEED_TOP) * has[side]
                speed[into, pl.ds(row, 8), :] = fast.reshape(8, 8, 128)[cut]
                slope[into, pl.ds(row, 8), :] = (fast * (1.0 + 2.0 * tilt)).reshape(8, 8, 128)[cut]
            fast = speed[7:15, pl.ds(row, 8), :]
            slope[7:15, pl.ds(row, 8), :] = fast * (1.0 + 2.0 * slope[7:15, pl.ds(row, 8), :])

    def open_far(j):
        @pl.loop(0, CHUNK)
        def _(i):
            k = CHUNK * j + i
            rows = pl.ds(pl.multiple_of(8 * k + 8, 8), 8)
            mids = []
            for f in range(4):
                at = CHUNK * f + i
                mids.append(spread(f, rows, far_in[0, j, at], far_in[1, j, at], z_in[j, at]))
            total[k] = (
                other_scale[0] * rounded(mids[1]) * snap_w[0, k]
                + own_scale[STEPS] * mids[3] * snap_u[STEPS, k].astype(jnp.float32)
            )

    def advance(phase, j):
        for n in range(1, STEPS + 1):
            first = jnp.maximum(CHUNK * j - n, 0)
            last = jnp.where(j == CHUNKS - 1, BLOCKS, jnp.maximum(CHUNK * j + CHUNK - n, 0))
            for w in range(2):
                @pl.loop(first, last)
                def _(k):
                    one_step(phase, w, n, k)

    fill_source(s)
    for side in range(2):
        rec_near_copy(1 - side).wait_recv()
    fill_records(rec_near, rec_near_in)

    @pl.loop(0, CHUNKS)
    def _(j):
        for side in range(2):
            near_copy(j, 1 - side).wait_recv()
        open_near(j)
        advance(0, j)

    rec_z_copy.wait_recv()
    for side in range(2):
        rec_far_copy(side).start()
    fill_source(across)
    for side in range(2):
        rec_far_copy(1 - side).wait_recv()
    fill_records(rec_z_in, rec_far_in)

    @pl.loop(0, CHUNKS + 1)
    def _(j):
        @pl.when(j < CHUNKS)
        def _():
            z_copy(j).wait_recv()
            for side in range(2):
                far_copy(j, side).start()

        @pl.when(j > 0)
        def _():
            for side in range(2):
                far_copy(j - 1, 1 - side).wait_recv()
            open_far(j - 1)
            advance(1, j - 1)

    def sum_copy(k):
        part = lax.rem(s + k, 8)
        src = total.at[pl.ds(half + 4 * part, 4)]
        return remote(src, sums.at[k - 1], sum_send.at[k - 1], sum_recv.at[k - 1], (8 * half + part, q))

    for k in range(1, 8):
        sum_copy(k).start()
    mine = half + 4 * lax.rem(s, 8)
    for k in range(1, 8):
        sum_copy(k).wait_recv()
    for i in range(4):
        value = total[mine + i]
        for k in range(7):
            value = value + sums[k, i]
        out[:, 8 * i : 8 * i + 8, :] = value.reshape(8, 8, 128)

    @pl.loop(0, CHUNKS)
    def _(j):
        z_copy(j).wait_send()
        for side in range(2):
            near_copy(j, side).wait_send()
            far_copy(j, side).wait_send()

    rec_z_copy.wait_send()
    for side in range(2):
        rec_near_copy(side).wait_send()
        rec_far_copy(side).wait_send()
    for k in range(1, 8):
        sum_copy(k).wait_send()


def on_device(*args):
    f32, i16 = jnp.float32, jnp.int16
    dma = pltpu.SemaphoreType.DMA
    fields = (args[0], args[1], args[2], args[3])
    records, speed, shape = args[4], args[5], args[6]
    anywhere, smem = pl.BlockSpec(memory_space=pl.ANY), pl.BlockSpec(memory_space=pltpu.SMEM)
    vmem = pl.BlockSpec(memory_space=pltpu.VMEM)
    return pl.pallas_call(
        kernel,
        out_shape=jax.ShapeDtypeStruct((8, 32, 128), f32),
        in_specs=[anywhere] * 6 + [vmem] + [smem] * 5,
        out_specs=vmem,
        scratch_shapes=[
            pltpu.VMEM((4, WIDE, ROWS + 16, 128), f32),
            pltpu.VMEM((WIDE, ROWS, 128), f32),
            pltpu.VMEM((WIDE, ROWS, 128), f32),
            pltpu.VMEM((8, BLOCKS, 64, 128), jnp.bfloat16),
            pltpu.VMEM((8, BLOCKS, 64, 128), f32),
            pltpu.VMEM((BLOCKS, 64, 128), f32),
            pltpu.VMEM((4, 8, ROWS, 128), f32),
            pltpu.VMEM((CHUNKS, 4 * CHUNK, 64, 128), i16),
            pltpu.VMEM((CHUNKS, 4 * CHUNK, 64, 128), i16),
            pltpu.VMEM((CHUNKS, 6 * CHUNK, 64, 128), i16),
            pltpu.VMEM((2, CHUNKS, 6 * CHUNK, 64, 128), i16),
            pltpu.VMEM((2, CHUNKS, 4 * CHUNK, 64, 128), i16),
            pltpu.VMEM((2, 2, 272, 128), f32),
            pltpu.VMEM((16, 8, 512), f32),
            pltpu.VMEM((528, 128), f32),
            pltpu.VMEM((17, 16, 128), i16),
            pltpu.VMEM((17, 16, 128), i16),
            pltpu.VMEM((17, 16, 128), i16),
            pltpu.VMEM((2, 17, 16, 128), i16),
            pltpu.VMEM((2, 17, 16, 128), i16),
            pltpu.VMEM((7, 4, 64, 128), f32),
            dma((10,)),
            dma((CHUNKS,)),
            dma((CHUNKS,)),
            dma((2, CHUNKS)),
            dma((2, CHUNKS)),
            dma((2, CHUNKS)),
            dma((2, CHUNKS)),
            dma,
            dma,
            dma((2,)),
            dma((2,)),
            dma((2,)),
            dma((2,)),
            dma((7,)),
            dma((7,)),
        ],
        compiler_params=pltpu.CompilerParams(
            collective_id=0, has_side_effects=True, vmem_limit_bytes=62 * 1024 * 1024
        ),
    )(*fields, speed, shape, records, *args[7:])


def solution(mesh):
    in_specs = (
        P("shot", "xy", None, None),
        P("shot", "xy", None, None),
        P("shot", "xy", None, None),
        P("shot", "xy", None, None),
        P("shot", None, "xy", None),
        P("xy", None, None),
        P("xy", None, None),
        P(),
        P(),
        P(),
        P(),
        P(),
    )
    return jax.shard_map(
        on_device, mesh=mesh, in_specs=in_specs, out_specs=P("xy", "shot", None), check_vma=False
    )
```

time: 701 us -> 214 us (0.31); the launches traced: 693 us -> 214 us
  waiting for transfers between devices: 268 us -> 0 us
  Pallas kernels: 0 us -> 209 us
  local copies, waits for them, and re-layouts: 145 us -> 4.28 us
  other arithmetic: 129 us -> 0 us
  starting transfers between devices: 106 us -> 0 us
  loops' own time: 26.8 us -> 0 us
  between operations: 18.3 us -> 0.01 us
    pallas_call x0 -> x1, Pallas kernels: none -> 209 us  [on_device(): pl.pallas_call(kernel, out_shape=jax.ShapeDtypeStruct((8, 32, 128), f32),...]
    ppermute x29 -> x0, waiting for transfers between devices: 162 us -> none  [the longest x1 162 us: passed_along(): return lax.ppermute(block, axis, route)]
    reduce_scatter x1 -> x0, waiting for transfers between devices: 106 us -> none  [on_device(): lax.psum_scatter(partial_value * inside, 'shot', scatter_dimension=1, til...]
    ppermute x29 -> x0, starting transfers between devices: 106 us -> none  [the longest x14 81.4 us: padded_2(): before = lax.ppermute(last, axis, up)]
    add x15 -> x0, other arithmetic: 74.6 us -> none  [the longest x7 45.2 us: correlate(): return partial_value + jnp.where(found, taken * field, 0.0)]
    dynamic_slice x35 -> x0, local copies, waits for them, and re-layouts: 62.4 us -> none  [the longest x14 29.1 us: record(): older = lax.dynamic_slice_in_dim(snaps, slot, 1, 0)]
    while x45 -> x0, local copies, waits for them, and re-layouts: 27.2 us -> none
    another operation x2 -> x0, loops' own time: 26.8 us -> none  [march(): return lax.fori_loop(0, step_count - 1, one_step, (before, current, state))]
  transfers between devices with their start and end apart: 30 -> 0, of which waited for: 2 -> 0; matrix products, arithmetic and copies ran while one was open for 17% -> 0% of each run, Pallas kernels for 0% -> 0%
where the time goes in v1:
time: 214 us
  Pallas kernels  209 us (98%)
  local copies, waits for them, and re-layouts  4.28 us (2%)
    pallas_call x1, Pallas kernels, on_device(): pl.pallas_call(kernel, out_shape=jax.ShapeDtypeStruct((8, 32, 128), f32),...  209 us

profile of v1, /device:TPU:40, one launch (start us, length us, event | category | flops | bytes accessed | tf_op | source)
XLA Modules:
  0.0 213.6 jit_solution(11522841499977446014)
XLA Ops:
  0.0 1.4 copy.13.wavelet
  1.4 1.4 copy.14.aperture
  2.7 209.3 %shard_map.118 = f32[8,32,128]{2,1,0:T(8,128)} custom-call(f32[1,8,512,128]{3,2,1,0:T(8,128)} %fields0.1, f32[1,8,512,128]{3,2,1,0:T(8,128)} %fields1.1, f32[1,8,512,128]{3,2,1,0:T(8,128)} %fields2.1, f32[1,8,512,128]{3,2,1,0:T(8,128)} %fields3.1, f32[8,512,128]{2,1,0:T(8,128)} %speed_hbm.1, f32[8,512,128]{2,1,0:T(8,128)} %shape_hbm.1, ...), custom_call_target="tpu_custom_call" | custom-call | tf_op jit(solution)/shard_map/pallas_call | solution.py:357
  212.0 1.6 copy.16

commit v2 on v1

--- a/solution.py
+++ b/solution.py
@@ -14,11 +14,14 @@
 CHUNKS = BLOCKS // CHUNK
 ROWS = 8 * BLOCKS
 STEPS = 7
+SENT_EARLY = 6
+AHEAD = 3
 WIDE = 22
 FIELD_TOP = 6.0
 RECORD_TOP = 12.0
 SPEED_TOP = 0.25
 SHAPE_TOP = 0.3
+SUM_TOP = 2.0**30
 
 
 def root_code(x, top):
@@ -32,6 +35,22 @@
     return (part * part) * (part * jnp.abs(part)) * top
 
 
+def long_code(x):
+    size = jnp.abs(x) * (1.0 / SUM_TOP)
+    for _ in range(4):
+        size = jnp.sqrt(size)
+    size = jnp.minimum(jnp.round(size * TOP), TOP)
+    return jnp.where(x < 0.0, -size, size).astype(jnp.int32).astype(jnp.int16)
+
+
+def long_value(code):
+    part = code.astype(jnp.int32).astype(jnp.float32) * (1.0 / TOP)
+    power = jnp.abs(part)
+    for _ in range(4):
+        power = power * power
+    return jnp.where(part < 0.0, -power, power) * SUM_TOP
+
+
 def line_code(x, top):
     return jnp.round(x * (TOP / top)).astype(jnp.int32).astype(jnp.int16)
 
@@ -44,7 +63,7 @@
     fields0, fields1, fields2, fields3, speed_hbm, shape_hbm, records, wavelet, shot_x, shot_y, aperture, snap_steps,
     out,
     state, slope, speed, snap_u, snap_w, total, stage, z_out, z_in, near, near_in, far_in,
-    inject, marks, turned, rec_z, rec_near, rec_z_in, rec_near_in, rec_far_in, sums,
+    inject, marks, turned, rec_z, rec_near, rec_z_in, rec_near_in, rec_far_in, sum_out, sums,
     in_sem, z_send, z_recv, near_send, near_recv, far_send, far_recv,
     rz_send, rz_recv, rn_send, rn_recv, rf_send, rf_recv, sum_send, sum_recv,
 ):
@@ -64,7 +83,7 @@
         loads.append(pltpu.make_async_copy(fields[f].at[0, :, pl.ds(base, ROWS), :], state.at[f, pl.ds(7, 8), pl.ds(8, ROWS), :], in_sem.at[4 + f]))
     loads.append(pltpu.make_async_copy(shape_hbm.at[:, pl.ds(base, ROWS), :], slope.at[pl.ds(7, 8)], in_sem.at[8]))
     loads.append(pltpu.make_async_copy(speed_hbm.at[:, pl.ds(base, ROWS), :], speed.at[pl.ds(7, 8)], in_sem.at[9]))
-    for load in loads:
+    for load in loads[:4]:
         load.start()
 
     barrier = pltpu.get_barrier_semaphore()
@@ -99,18 +118,45 @@
 
     rec_z_copy = remote(rec_z, rec_z_in, rz_send, rz_recv, (across, q))
 
-    for load in loads[:4]:
-        load.wait()
-    pl.semaphore_wait(barrier, len(peers))
-
-    @pl.loop(0, CHUNKS)
-    def _(j):
+    def encode(j):
         for f in range(4):
             for i in range(CHUNK):
                 row = pl.multiple_of(8 * (CHUNK * j + i), 8)
                 block = stage[f, :, pl.ds(row, 8), :].reshape(64, 128)
                 z_out[j, CHUNK * f + i] = root_code(block, FIELD_TOP)
-        z_copy(j).start()
+
+    for load in loads[:4]:
+        load.wait()
+    for load in loads[4:]:
+        load.start()
+    encode(0)
+    pl.semaphore_wait(barrier, len(peers))
+    z_copy(0).start()
+
+    marks[...] = jnp.zeros_like(marks)
+    for t in range(STEPS):
+        for x in range(8):
+            marks[x, t : t + 1, :] = records[0, t, x : x + 1, :]
+    turned[pl.ds(512, 16)] = jnp.zeros((16, 128), jnp.float32)
+    turned[pl.ds(0, 512)] = jnp.transpose(marks[...].reshape(128, 512), (1, 0))
+
+    @pl.loop(0, 17)
+    def _(k):
+        row = 16 * k
+        rec_z[k] = root_code(turned[pl.ds(pl.multiple_of(their_base + row, 8), 16), :], RECORD_TOP)
+        rec_near[k] = root_code(turned[pl.ds(pl.multiple_of(base + row, 8), 16), :], RECORD_TOP)
+
+    rec_z_copy.start()
+    for side in range(2):
+        rec_near_copy(side).start()
+
+    @pl.loop(1, CHUNKS)
+    def _(j):
+        encode(j)
+
+        @pl.when(j < AHEAD)
+        def _():
+            z_copy(j).start()
 
     for load in loads[4:]:
         load.wait()
@@ -127,23 +173,6 @@
         for side in range(2):
             near_copy(j, side).start()
 
-    marks[...] = jnp.zeros_like(marks)
-    for t in range(STEPS):
-        for x in range(8):
-            marks[x, t : t + 1, :] = records[0, t, x : x + 1, :]
-    turned[pl.ds(512, 16)] = jnp.zeros((16, 128), jnp.float32)
-    turned[pl.ds(0, 512)] = jnp.transpose(marks[...].reshape(128, 512), (1, 0))
-
-    @pl.loop(0, 17)
-    def _(k):
-        row = 16 * k
-        rec_z[k] = root_code(turned[pl.ds(pl.multiple_of(their_base + row, 8), 16), :], RECORD_TOP)
-        rec_near[k] = root_code(turned[pl.ds(pl.multiple_of(base + row, 8), 16), :], RECORD_TOP)
-
-    rec_z_copy.start()
-    for side in range(2):
-        rec_near_copy(side).start()
-
     lane = lax.broadcasted_iota(jnp.int32, (8, 128), 1)
     sub = lax.broadcasted_iota(jnp.int32, (8, 128), 0)
     wide_lane = lax.broadcasted_iota(jnp.int32, (16, 128), 1)
@@ -152,7 +181,7 @@
     def fill_source(shot):
         tag = jnp.zeros((8, 128), jnp.float32)
         for t in range(STEPS):
-            tag = jnp.where((lane & 7) == t, wavelet[shot, t], tag)
+            tag = jnp.where((lane & 7) == t, wavelet[t, shot], tag)
         at_x = shot_x[shot] - 8 * q + 7
         at_y = shot_y[shot] - base
 
@@ -180,7 +209,7 @@
     def imaged(shot):
         inside = jnp.float32(0.0)
         for i in range(8):
-            inside = inside + jnp.where(aperture[shot, i] == q, 1.0, 0.0)
+            inside = inside + jnp.where(aperture[i, shot] == q, 1.0, 0.0)
         scale = []
         for t in range(1, 9):
             hit = jnp.float32(0.0)
@@ -194,43 +223,51 @@
     def rounded(x):
         return x.astype(jnp.bfloat16).astype(jnp.float32)
 
-    def one_step(phase, w, n, k):
-        old, now = 2 * w + (n - 1) % 2, 2 * w + n % 2
-        entry = n - 1 if w == 0 else STEPS - n
+    def layers(n, size):
+        found = []
+        for low, high in ((n, 7), (7, 15), (15, WIDE - n)):
+            found += [(x, min(x + size, high)) for x in range(low, high, size)]
+        return found
+
+    def one_step(phase, n, k, blocks, size):
+        tall = 8 * blocks
         row = pl.multiple_of(8 * k, 8)
-        here = pl.ds(pl.multiple_of(row + 8, 8), 8)
-        groups = [(7, 15)] if n == STEPS else [(n, 7), (7, 15), (15, WIDE - n)]
-        for x0, x1 in groups:
+        here, flat_here = pl.ds(pl.multiple_of(row + 8, 8), tall), pl.ds(row, tall)
+        for x0, x1 in layers(n, size):
             count = x1 - x0
-            big = state[now, x0 - 1 : x1 + 1, here, :]
-            mid = big[1:-1]
-            lateral = big[:-2] + big[2:]
-            lateral = lateral + state[now, x0:x1, pl.ds(row + 7, 8), :]
-            lateral = lateral + state[now, x0:x1, pl.ds(row + 9, 8), :]
-            lateral = lateral - 4.0 * mid
-            sources = [inject[w, g, pl.ds(row, 8), :] for g in range(2)]
-            added = jnp.stack([
-                pltpu.roll(sources[x // 16], (128 - 8 * (x % 16) - entry) % 128, 1) for x in range(x0, x1)
-            ])
-            at = lax.broadcasted_iota(jnp.int32, (count, 8, 128), 2)
-            up = jnp.where(at == 0, added, pltpu.roll(mid, 1, 2))
-            down = jnp.where(at == 127, 0.0, pltpu.roll(mid, 127, 2))
-            twice = 2.0 * mid
-            vertical = up + down - twice
-            new = twice - state[old, x0:x1, here, :]
-            new = new + slope[x0:x1, pl.ds(row, 8), :] * lateral + speed[x0:x1, pl.ds(row, 8), :] * vertical
-            state[old, x0:x1, here, :] = new
-            if x0 == 7:
-                flat = new.reshape(64, 128)
-                if phase == 0 and w == 0:
-                    snap_u[n, k] = flat.astype(jnp.bfloat16)
-                elif phase == 0:
-                    snap_w[STEPS - n, k] = flat
-                elif w == 0:
-                    total[k] += other_scale[n] * rounded(flat) * snap_w[n, k]
-                else:
-                    level = STEPS - n
-                    total[k] += own_scale[level] * flat * snap_u[level, k].astype(jnp.float32)
+            at = lax.broadcasted_iota(jnp.int32, (count, tall, 128), 2)
+            for w in range(2):
+                old, now = 2 * w + (n - 1) % 2, 2 * w + n % 2
+                entry = n - 1 if w == 0 else STEPS - n
+                big = state[now, x0 - 1 : x1 + 1, here, :]
+                mid = big[1:-1]
+                lateral = big[:-2] + big[2:]
+                beside = state[now, x0:x1, pl.ds(row + 7, tall), :] + state[now, x0:x1, pl.ds(row + 9, tall), :]
+                lateral = lateral + beside - 4.0 * mid
+                added = jnp.stack([
+                    pltpu.roll(inject[w, x // 16, flat_here, :], (128 - 8 * (x % 16) - entry) % 128, 1)
+                    for x in range(x0, x1)
+                ])
+                up = jnp.where(at == 0, added, pltpu.roll(mid, 1, 2))
+                down = jnp.where(at == 127, 0.0, pltpu.roll(mid, 127, 2))
+                twice = 2.0 * mid
+                new = twice - state[old, x0:x1, here, :]
+                new = new + slope[x0:x1, flat_here, :] * lateral + speed[x0:x1, flat_here, :] * (up + down - twice)
+                state[old, x0:x1, here, :] = new
+                if not 7 <= x0 < 15:
+                    continue
+                for i in range(blocks):
+                    flat = new[:, 8 * i : 8 * i + 8, :].reshape(8 * count, 128)
+                    part = pl.ds(8 * (x0 - 7), 8 * count)
+                    if phase == 0 and w == 0:
+                        snap_u[n, k + i, part] = flat.astype(jnp.bfloat16)
+                    elif phase == 0:
+                        snap_w[STEPS - n, k + i, part] = flat
+                    elif w == 0:
+                        total[k + i, part] += other_scale[n] * rounded(flat) * snap_w[n, k + i, part]
+                    else:
+                        level = STEPS - n
+                        total[k + i, part] += own_scale[level] * flat * snap_u[level, k + i, part].astype(jnp.float32)
 
     def spread(f, rows, low, high, mid=None):
         state[f, 0:7, rows, :] = (root_value(low, FIELD_TOP) * has[0]).reshape(8, 8, 128)[1:8]
@@ -276,10 +313,28 @@
         for n in range(1, STEPS + 1):
             first = jnp.maximum(CHUNK * j - n, 0)
             last = jnp.where(j == CHUNKS - 1, BLOCKS, jnp.maximum(CHUNK * j + CHUNK - n, 0))
-            for w in range(2):
-                @pl.loop(first, last)
-                def _(k):
-                    one_step(phase, w, n, k)
+            threes = (last - first) // CHUNK
+
+            @pl.loop(0, threes)
+            def _(i):
+                one_step(phase, n, first + CHUNK * i, CHUNK, 4)
+
+            @pl.loop(first + CHUNK * threes, last)
+            def _(k):
+                one_step(phase, n, k, 1, 8)
+
+    mine = lax.rem(s, 8)
+
+    def sum_copy(k):
+        part = lax.rem(s + k, 8)
+        return remote(sum_out.at[part], sums.at[k - 1], sum_send.at[k - 1], sum_recv.at[k - 1], (8 * half + part, q))
+
+    def send_sums(part):
+        @pl.when(part != mine)
+        def _():
+            for i in range(4):
+                sum_out[part, i] = long_code(total[half + 4 * part + i])
+            sum_copy(lax.rem(part - mine + 8, 8)).start()
 
     fill_source(s)
     for side in range(2):
@@ -292,6 +347,11 @@
             near_copy(j, 1 - side).wait_recv()
         open_near(j)
         advance(0, j)
+
+        @pl.when((lax.rem(j, 3) == 2) & (j // 3 + AHEAD < SENT_EARLY))
+        def _():
+            z_copy(j // 3).wait_send()
+            z_copy(j // 3 + AHEAD).start()
 
     rec_z_copy.wait_recv()
     for side in range(2):
@@ -309,32 +369,38 @@
             for side in range(2):
                 far_copy(j, side).start()
 
+        @pl.when((j >= SENT_EARLY - 2) & (j < CHUNKS - 2))
+        def _():
+            z_copy(j).wait_send()
+            z_copy(j + 2).start()
+
         @pl.when(j > 0)
         def _():
             for side in range(2):
                 far_copy(j - 1, 1 - side).wait_recv()
             open_far(j - 1)
             advance(1, j - 1)
-
-    def sum_copy(k):
-        part = lax.rem(s + k, 8)
-        src = total.at[pl.ds(half + 4 * part, 4)]
-        return remote(src, sums.at[k - 1], sum_send.at[k - 1], sum_recv.at[k - 1], (8 * half + part, q))
-
-    for k in range(1, 8):
-        sum_copy(k).start()
-    mine = half + 4 * lax.rem(s, 8)
+        for part, ready in ((0, 5), (2, 7)):
+            @pl.when(j - 1 == ready)
+            def _():
+                send_sums(part)
+                send_sums(part + 1)
+
+    for part in range(4, 8):
+        send_sums(part)
     for k in range(1, 8):
         sum_copy(k).wait_recv()
     for i in range(4):
-        value = total[mine + i]
+        value = total[half + 4 * mine + i]
         for k in range(7):
-            value = value + sums[k, i]
+            value = value + long_value(sums[k, i])
         out[:, 8 * i : 8 * i + 8, :] = value.reshape(8, 8, 128)
 
     @pl.loop(0, CHUNKS)
     def _(j):
-        z_copy(j).wait_send()
+        @pl.when(((j >= SENT_EARLY - AHEAD) & (j < SENT_EARLY - 2)) | (j >= CHUNKS - 2))
+        def _():
+            z_copy(j).wait_send()
         for side in range(2):
             near_copy(j, side).wait_send()
             far_copy(j, side).wait_send()
@@ -380,7 +446,8 @@
             pltpu.VMEM((17, 16, 128), i16),
             pltpu.VMEM((2, 17, 16, 128), i16),
             pltpu.VMEM((2, 17, 16, 128), i16),
-            pltpu.VMEM((7, 4, 64, 128), f32),
+            pltpu.VMEM((8, 4, 64, 128), i16),
+            pltpu.VMEM((7, 4, 64, 128), i16),
             dma((10,)),
             dma((CHUNKS,)),
             dma((CHUNKS,)),
@@ -400,7 +467,7 @@
         compiler_params=pltpu.CompilerParams(
             collective_id=0, has_side_effects=True, vmem_limit_bytes=62 * 1024 * 1024
         ),
-    )(*fields, speed, shape, records, *args[7:])
+    )(*fields, speed, shape, records, args[7].T, args[8], args[9], args[10].T, args[11])
 
 
 def solution(mesh):

time: 214 us -> 152 us (0.71)
  Pallas kernels: 209 us -> 149 us
  local copies, waits for them, and re-layouts: 4.28 us -> 1.57 us
    pallas_call x1, Pallas kernels: 209 us -> 149 us  [on_device(): pl.pallas_call(kernel, out_shape=jax.ShapeDtypeStruct((8, 32, 128), f32),...]
    unnamed x3 -> x1, local copies, waits for them, and re-layouts: 4.28 us -> 1.57 us
where the time goes in v2:
time: 152 us; the launch traced here: 151 us
  Pallas kernels  149 us (98%)
  local copies, waits for them, and re-layouts  1.57 us (1%)
    pallas_call x1, Pallas kernels, on_device(): pl.pallas_call(kernel, out_shape=jax.ShapeDtypeStruct((8, 32, 128), f32),...  149 us

profile of v2, /device:TPU:40, one launch (start us, length us, event | category | flops | bytes accessed | tf_op | source)
XLA Modules:
  0.0 150.7 jit_solution(15946440081331915995)
XLA Ops:
  0.0 149.1 %shard_map.118 = f32[8,32,128]{2,1,0:T(8,128)} custom-call(f32[1,8,512,128]{3,2,1,0:T(8,128)} %fields0.1, f32[1,8,512,128]{3,2,1,0:T(8,128)} %fields1.1, f32[1,8,512,128]{3,2,1,0:T(8,128)} %fields2.1, f32[1,8,512,128]{3,2,1,0:T(8,128)} %fields3.1, f32[8,512,128]{2,1,0:T(8,128)} %speed_hbm.1, f32[8,512,128]{2,1,0:T(8,128)} %shape_hbm.1, ...), custom_call_target="tpu_custom_call" | custom-call | tf_op jit(solution)/shard_map/pallas_call | solution.py:423
  149.1 1.6 %copy.14 = f32[8,32,128]{2,1,0:T(8,128)} copy(f32[8,32,128]{2,1,0:T(8,128)} %shard_map.118) | data formatting | bytes 262144

commit v3 on v2

--- a/solution.py
+++ b/solution.py
@@ -14,8 +14,9 @@
 CHUNKS = BLOCKS // CHUNK
 ROWS = 8 * BLOCKS
 STEPS = 7
-SENT_EARLY = 6
-AHEAD = 3
+BESIDE = 5
+SENT_EARLY = 8
+AHEAD = 5
 WIDE = 22
 FIELD_TOP = 6.0
 RECORD_TOP = 12.0
@@ -76,14 +77,18 @@
     base = pl.multiple_of(248 * half, 8)
     their_base = pl.multiple_of(248 * (1 - half), 8)
 
-    loads = []
+    firsts, loads = [], []
+    tall = 8 * CHUNK
     for f in range(4):
-        loads.append(pltpu.make_async_copy(fields[f].at[0, :, pl.ds(their_base, ROWS), :], stage.at[f], in_sem.at[f]))
+        theirs = fields[f].at[0]
+        rest = pl.ds(pl.multiple_of(their_base + tall, 8), ROWS - tall)
+        firsts.append(pltpu.make_async_copy(theirs.at[:, pl.ds(their_base, tall), :], stage.at[f, :, pl.ds(0, tall), :], in_sem.at[10 + f]))
+        loads.append(pltpu.make_async_copy(theirs.at[:, rest, :], stage.at[f, :, pl.ds(tall, ROWS - tall), :], in_sem.at[f]))
     for f in range(4):
         loads.append(pltpu.make_async_copy(fields[f].at[0, :, pl.ds(base, ROWS), :], state.at[f, pl.ds(7, 8), pl.ds(8, ROWS), :], in_sem.at[4 + f]))
     loads.append(pltpu.make_async_copy(shape_hbm.at[:, pl.ds(base, ROWS), :], slope.at[pl.ds(7, 8)], in_sem.at[8]))
     loads.append(pltpu.make_async_copy(speed_hbm.at[:, pl.ds(base, ROWS), :], speed.at[pl.ds(7, 8)], in_sem.at[9]))
-    for load in loads[:4]:
+    for load in firsts + loads[:4]:
         load.start()
 
     barrier = pltpu.get_barrier_semaphore()
@@ -125,7 +130,7 @@
                 block = stage[f, :, pl.ds(row, 8), :].reshape(64, 128)
                 z_out[j, CHUNK * f + i] = root_code(block, FIELD_TOP)
 
-    for load in loads[:4]:
+    for load in firsts:
         load.wait()
     for load in loads[4:]:
         load.start()
@@ -149,6 +154,9 @@
     rec_z_copy.start()
     for side in range(2):
         rec_near_copy(side).start()
+
+    for load in loads[:4]:
+        load.wait()
 
     @pl.loop(1, CHUNKS)
     def _(j):
@@ -329,12 +337,11 @@
         part = lax.rem(s + k, 8)
         return remote(sum_out.at[part], sums.at[k - 1], sum_send.at[k - 1], sum_recv.at[k - 1], (8 * half + part, q))
 
-    def send_sums(part):
-        @pl.when(part != mine)
-        def _():
-            for i in range(4):
-                sum_out[part, i] = long_code(total[half + 4 * part + i])
-            sum_copy(lax.rem(part - mine + 8, 8)).start()
+    def send_sums(k):
+        part = lax.rem(s + k, 8)
+        for i in range(4):
+            sum_out[part, i] = long_code(total[half + 4 * part + i])
+        sum_copy(k).start()
 
     fill_source(s)
     for side in range(2):
@@ -356,6 +363,16 @@
     rec_z_copy.wait_recv()
     for side in range(2):
         rec_far_copy(side).start()
+
+    def pass_on(j):
+        z_copy(j).wait_recv()
+        for side in range(2):
+            far_copy(j, side).start()
+
+    @pl.loop(0, BESIDE)
+    def _(j):
+        pass_on(j)
+
     fill_source(across)
     for side in range(2):
         rec_far_copy(1 - side).wait_recv()
@@ -363,11 +380,9 @@
 
     @pl.loop(0, CHUNKS + 1)
     def _(j):
-        @pl.when(j < CHUNKS)
-        def _():
-            z_copy(j).wait_recv()
-            for side in range(2):
-                far_copy(j, side).start()
+        @pl.when((j >= BESIDE) & (j < CHUNKS))
+        def _():
+            pass_on(j)
 
         @pl.when((j >= SENT_EARLY - 2) & (j < CHUNKS - 2))
         def _():
@@ -380,21 +395,15 @@
                 far_copy(j - 1, 1 - side).wait_recv()
             open_far(j - 1)
             advance(1, j - 1)
-        for part, ready in ((0, 5), (2, 7)):
-            @pl.when(j - 1 == ready)
-            def _():
-                send_sums(part)
-                send_sums(part + 1)
-
-    for part in range(4, 8):
-        send_sums(part)
-    for k in range(1, 8):
+
+    for k in (4, 3, 5, 2, 6, 1, 7):
+        send_sums(k)
+    for k in (1, 7, 2, 6, 3, 5, 4):
         sum_copy(k).wait_recv()
+        for i in range(4):
+            total[half + 4 * mine + i] += long_value(sums[k - 1, i])
     for i in range(4):
-        value = total[half + 4 * mine + i]
-        for k in range(7):
-            value = value + long_value(sums[k, i])
-        out[:, 8 * i : 8 * i + 8, :] = value.reshape(8, 8, 128)
+        out[:, 8 * i : 8 * i + 8, :] = total[half + 4 * mine + i].reshape(8, 8, 128)
 
     @pl.loop(0, CHUNKS)
     def _(j):
@@ -448,7 +457,7 @@
             pltpu.VMEM((2, 17, 16, 128), i16),
             pltpu.VMEM((8, 4, 64, 128), i16),
             pltpu.VMEM((7, 4, 64, 128), i16),
-            dma((10,)),
+            dma((14,)),
             dma((CHUNKS,)),
             dma((CHUNKS,)),
             dma((2, CHUNKS)),

time: 152 us -> 136 us (0.89); the launches traced: 151 us -> 136 us
  Pallas kernels: 149 us -> 135 us
    pallas_call x1, Pallas kernels: 149 us -> 135 us  [on_device(): pl.pallas_call(kernel, out_shape=jax.ShapeDtypeStruct((8, 32, 128), f32),...]
where the time goes in v3:
time: 136 us
  Pallas kernels  135 us (99%)
  local copies, waits for them, and re-layouts  1.57 us (1%)
    pallas_call x1, Pallas kernels, on_device(): pl.pallas_call(kernel, out_shape=jax.ShapeDtypeStruct((8, 32, 128), f32),...  135 us

profile of v3, /device:TPU:40, one launch (start us, length us, event | category | flops | bytes accessed | tf_op | source)
XLA Modules:
  0.0 136.3 jit_solution(10750519464119106402)
XLA Ops:
  0.0 134.7 %shard_map.118 = f32[8,32,128]{2,1,0:T(8,128)} custom-call(f32[1,8,512,128]{3,2,1,0:T(8,128)} %fields0.1, f32[1,8,512,128]{3,2,1,0:T(8,128)} %fields1.1, f32[1,8,512,128]{3,2,1,0:T(8,128)} %fields2.1, f32[1,8,512,128]{3,2,1,0:T(8,128)} %fields3.1, f32[8,512,128]{2,1,0:T(8,128)} %speed_hbm.1, f32[8,512,128]{2,1,0:T(8,128)} %shape_hbm.1, ...), custom_call_target="tpu_custom_call" | custom-call | tf_op jit(solution)/shard_map/pallas_call | solution.py:432
  134.7 1.6 %copy.14 = f32[8,32,128]{2,1,0:T(8,128)} copy(f32[8,32,128]{2,1,0:T(8,128)} %shard_map.118) | data formatting | bytes 262144

commit v4 on v3

--- a/solution.py
+++ b/solution.py
@@ -148,8 +148,15 @@
     @pl.loop(0, 17)
     def _(k):
         row = 16 * k
-        rec_z[k] = root_code(turned[pl.ds(pl.multiple_of(their_base + row, 8), 16), :], RECORD_TOP)
         rec_near[k] = root_code(turned[pl.ds(pl.multiple_of(base + row, 8), 16), :], RECORD_TOP)
+
+    wide_lane = lax.broadcasted_iota(jnp.int32, (16, 128), 1)
+
+    @pl.loop(0, 9)
+    def _(k):
+        low = turned[pl.ds(pl.multiple_of(their_base + 16 * k, 8), 16), :]
+        high = turned[pl.ds(pl.multiple_of(their_base + 136 + 16 * k, 8), 16), :]
+        rec_z[k] = root_code(jnp.where(wide_lane < 64, low, pltpu.roll(high, 64, 1)), RECORD_TOP)
 
     rec_z_copy.start()
     for side in range(2):
@@ -183,7 +190,6 @@
 
     lane = lax.broadcasted_iota(jnp.int32, (8, 128), 1)
     sub = lax.broadcasted_iota(jnp.int32, (8, 128), 0)
-    wide_lane = lax.broadcasted_iota(jnp.int32, (16, 128), 1)
     has = (jnp.where(q > 0, 1.0, 0.0), jnp.where(q < 15, 1.0, 0.0))
 
     def fill_source(shot):
@@ -200,15 +206,29 @@
                 hit = ((sub + row) == at_y) & (((lane >> 3) + 16 * g) == at_x)
                 inject[0, g, pl.ds(row, 8), :] = jnp.where(hit, tag, 0.0)
 
-    def fill_records(middle, beside):
+    def place_records(row, parts):
+        low = pltpu.roll(parts[0], 120, 1) * has[0]
+        mid = pltpu.roll(parts[1], 56, 1)
+        high = pltpu.roll(parts[2], 120, 1) * has[1]
+        inject[1, 0, pl.ds(row, 16), :] = jnp.where(wide_lane < 56, low, jnp.where(wide_lane < 120, mid, high))
+        inject[1, 1, pl.ds(row, 16), :] = high
+
+    def fill_near_records():
         @pl.loop(0, 17)
         def _(k):
-            row = pl.multiple_of(16 * k, 8)
-            low = pltpu.roll(root_value(beside[0, k], RECORD_TOP), 120, 1) * has[0]
-            mid = pltpu.roll(root_value(middle[k], RECORD_TOP), 56, 1)
-            high = pltpu.roll(root_value(beside[1, k], RECORD_TOP), 120, 1) * has[1]
-            inject[1, 0, pl.ds(row, 16), :] = jnp.where(wide_lane < 56, low, jnp.where(wide_lane < 120, mid, high))
-            inject[1, 1, pl.ds(row, 16), :] = high
+            codes = (rec_near_in[0, k], rec_near[k], rec_near_in[1, k])
+            place_records(pl.multiple_of(16 * k, 8), [root_value(c, RECORD_TOP) for c in codes])
+
+    def fill_far_records():
+        @pl.loop(0, 9)
+        def _(k):
+            parts = [root_value(c, RECORD_TOP) for c in (rec_far_in[0, k], rec_z_in[k], rec_far_in[1, k])]
+            place_records(pl.multiple_of(16 * k, 8), parts)
+
+        @pl.loop(0, 9)
+        def _(k):
+            parts = [root_value(c, RECORD_TOP) for c in (rec_far_in[0, k], rec_z_in[k], rec_far_in[1, k])]
+            place_records(pl.multiple_of(136 + 16 * k, 8), [pltpu.roll(p, 64, 1) for p in parts])
 
     for f in range(4):
         state[f, :, 0:8, :] = jnp.zeros((WIDE, 8, 128), jnp.float32)
@@ -346,7 +366,7 @@
     fill_source(s)
     for side in range(2):
         rec_near_copy(1 - side).wait_recv()
-    fill_records(rec_near, rec_near_in)
+    fill_near_records()
 
     @pl.loop(0, CHUNKS)
     def _(j):
@@ -376,7 +396,7 @@
     fill_source(across)
     for side in range(2):
         rec_far_copy(1 - side).wait_recv()
-    fill_records(rec_z_in, rec_far_in)
+    fill_far_records()
 
     @pl.loop(0, CHUNKS + 1)
     def _(j):
@@ -447,14 +467,14 @@
             pltpu.VMEM((CHUNKS, 6 * CHUNK, 64, 128), i16),
             pltpu.VMEM((2, CHUNKS, 6 * CHUNK, 64, 128), i16),
             pltpu.VMEM((2, CHUNKS, 4 * CHUNK, 64, 128), i16),
-            pltpu.VMEM((2, 2, 272, 128), f32),
+            pltpu.VMEM((2, 2, 280, 128), f32),
             pltpu.VMEM((16, 8, 512), f32),
             pltpu.VMEM((528, 128), f32),
+            pltpu.VMEM((9, 16, 128), i16),
             pltpu.VMEM((17, 16, 128), i16),
-            pltpu.VMEM((17, 16, 128), i16),
-            pltpu.VMEM((17, 16, 128), i16),
+            pltpu.VMEM((9, 16, 128), i16),
             pltpu.VMEM((2, 17, 16, 128), i16),
-            pltpu.VMEM((2, 17, 16, 128), i16),
+            pltpu.VMEM((2, 9, 16, 128), i16),
             pltpu.VMEM((8, 4, 64, 128), i16),
             pltpu.VMEM((7, 4, 64, 128), i16),
             dma((14,)),

time: 136 us -> 134 us (0.985)
  Pallas kernels: 135 us -> 133 us
    pallas_call x1, Pallas kernels: 135 us -> 133 us  [on_device(): pl.pallas_call(kernel, out_shape=jax.ShapeDtypeStruct((8, 32, 128), f32),...]
where the time goes in v4:
time: 134 us
  Pallas kernels  133 us (99%)
  local copies, waits for them, and re-layouts  1.57 us (1%)
    pallas_call x1, Pallas kernels, on_device(): pl.pallas_call(kernel, out_shape=jax.ShapeDtypeStruct((8, 32, 128), f32),...  133 us

profile of v4, /device:TPU:40, one launch (start us, length us, event | category | flops | bytes accessed | tf_op | source)
XLA Modules:
  0.0 134.1 jit_solution(69519118260491736)
XLA Ops:
  0.0 132.5 %shard_map.118 = f32[8,32,128]{2,1,0:T(8,128)} custom-call(f32[1,8,512,128]{3,2,1,0:T(8,128)} %fields0.1, f32[1,8,512,128]{3,2,1,0:T(8,128)} %fields1.1, f32[1,8,512,128]{3,2,1,0:T(8,128)} %fields2.1, f32[1,8,512,128]{3,2,1,0:T(8,128)} %fields3.1, f32[8,512,128]{2,1,0:T(8,128)} %speed_hbm.1, f32[8,512,128]{2,1,0:T(8,128)} %shape_hbm.1, ...), custom_call_target="tpu_custom_call" | custom-call | tf_op jit(solution)/shard_map/pallas_call | solution.py:452
  132.5 1.6 %copy.14 = f32[8,32,128]{2,1,0:T(8,128)} copy(f32[8,32,128]{2,1,0:T(8,128)} %shard_map.118) | data formatting | bytes 262144

commit v5 on v4

--- a/solution.py
+++ b/solution.py
@@ -15,8 +15,8 @@
 ROWS = 8 * BLOCKS
 STEPS = 7
 BESIDE = 5
-SENT_EARLY = 8
-AHEAD = 5
+SENT_EARLY = 9
+AHEAD = 6
 WIDE = 22
 FIELD_TOP = 6.0
 RECORD_TOP = 12.0

time: 134 us -> 135 us (level)
  the two profiles are of different devices: /device:TPU:40 before, /device:TPU:7 now
where the time goes in v5:
time: 135 us
  Pallas kernels  133 us (99%)
  local copies, waits for them, and re-layouts  1.57 us (1%)
    pallas_call x1, Pallas kernels, on_device(): pl.pallas_call(kernel, out_shape=jax.ShapeDtypeStruct((8, 32, 128), f32),...  133 us

profile of v5, /device:TPU:7, one launch (start us, length us, event | category | flops | bytes accessed | tf_op | source)
XLA Modules:
  0.0 135.0 jit_solution(1290845080104942120)
XLA Ops:
  0.0 133.5 %shard_map.118 = f32[8,32,128]{2,1,0:T(8,128)} custom-call(f32[1,8,512,128]{3,2,1,0:T(8,128)} %fields0.1, f32[1,8,512,128]{3,2,1,0:T(8,128)} %fields1.1, f32[1,8,512,128]{3,2,1,0:T(8,128)} %fields2.1, f32[1,8,512,128]{3,2,1,0:T(8,128)} %fields3.1, f32[8,512,128]{2,1,0:T(8,128)} %speed_hbm.1, f32[8,512,128]{2,1,0:T(8,128)} %shape_hbm.1, ...), custom_call_target="tpu_custom_call" | custom-call | tf_op jit(solution)/shard_map/pallas_call | solution.py:452
  133.5 1.6 %copy.14 = f32[8,32,128]{2,1,0:T(8,128)} copy(f32[8,32,128]{2,1,0:T(8,128)} %shard_map.118) | data formatting | bytes 262144
